TPU v7x, 256 devices: a whole 4x4x8 slice. The times are simulated.
256 devices in a mesh: ctx: 32 (over z, x_lo, core), head: 8 (over y, x_hi).
Axes of the slice: x: 4 (x_hi: 2, x_lo: 2; x = x_hi * 2 + x_lo), y: 4, z: 8, core: 2. Of those that a mesh axis runs over, the one named last changes fastest.
Arguments:
- q_latent: bfloat16 [4096, 1536], P('ctx'), may hold values from -6 to 6
- kv_latent: bfloat16 [4096, 576], P('ctx'), may hold values from -420 to 420
- q_gain: float32 [1536], replicated, may hold values from 0.1 to 1.9
- kv_gain: float32 [512], replicated, may hold values from 0.1 to 1.9
- q_up: bfloat16 [1536, 12288], P(None, 'head'), may hold values from -0.15625 to 0.15625
- kv_up: bfloat16 [512, 16384], P(None, 'head'), may hold values from -0.25 to 0.25
- out_proj: bfloat16 [8192, 7168], P(('head', 'ctx')), may hold values from -0.5 to 0.5
- segment_ids: int32 [4096], replicated, may hold values from 0 to 7, never falling along the last dimension, each value on 1 to 1024 neighbouring positions
- trace_limit: int32 [8], replicated, may hold values from 1 to 1024
Outputs:
- mixed: bfloat16 [4096, 7168], P('ctx', 'head')
Inputs may be any that keep to these rules, and one draw needn't show every extreme that they name: `segment_ids`: trace numbers never fall along the window; each trace holds 1 to 1024 tokens, one exactly 1024.
All inputs are finite; a program needn't handle non-finite values.
Results may differ from a plain program's by a relative error of at most 0.025.
The roundings to bfloat16 on the way count: a program that leaves them out, or rounds other values in their place, can miss the bound.
Values may be sent and summed in bfloat16 or wider, within the bound.
A program may use at most 128 MiB of HBM per device.

v0:
```python
import jax
import jax.numpy as jnp
from jax import lax
from jax.sharding import PartitionSpec as P

KV_RANK = 512
QK_NOPE = 128
QK_ROPE = 64
V_DIM = 128


def rms_scale(values, gain):
    return values * lax.rsqrt(jnp.mean(values * values, axis=-1, keepdims=True) + 1e-06) * gain


def rotate(values, places):
    half = values.shape[-1] // 2
    inverse = 10000.0 ** (-jnp.arange(half, dtype=jnp.float32) / half)
    angles = places.astype(jnp.float32)[:, None] * inverse[None, :]
    cosine = jnp.cos(angles)
    sine = jnp.sin(angles)
    if values.ndim == 3:
        cosine = cosine[:, None, :]
        sine = sine[:, None, :]
    first = values[..., :half]
    second = values[..., half:]
    return jnp.concatenate(
        [first * cosine - second * sine, first * sine + second * cosine], axis=-1
    )


def token_flags(segment_ids, trace_limit):
    traces = trace_limit.shape[0]
    count = segment_ids.shape[0]
    numbers = jnp.arange(traces, dtype=jnp.int32)
    onehot = (segment_ids[:, None] == numbers[None, :]).astype(jnp.int32)
    before = (segment_ids[:, None] < numbers[None, :]).astype(jnp.int32)
    starts = jnp.sum(before, axis=0)
    start_tok = jnp.sum(onehot * starts[None, :], axis=1)
    limit_tok = jnp.sum(onehot * trace_limit[None, :], axis=1)
    place = jnp.arange(count, dtype=jnp.int32) - start_tok
    return place < limit_tok


def keep_state(state):
    return state


def body(q_latent, kv_latent, q_gain, kv_gain, q_up, kv_up, out_proj, segment_ids, trace_limit):
    rows = q_latent.shape[0]
    offset = lax.axis_index("ctx") * rows
    places = offset + jnp.arange(rows, dtype=jnp.int32)
    heads = q_up.shape[1] // (QK_NOPE + QK_ROPE)
    qnorm = rms_scale(q_latent.astype(jnp.float32), q_gain).astype(jnp.bfloat16)
    qfull = jnp.dot(qnorm, q_up, preferred_element_type=jnp.float32).reshape(
        rows, heads, QK_NOPE + QK_ROPE
    )
    query = jnp.concatenate(
        [qfull[..., :QK_NOPE], rotate(qfull[..., QK_NOPE:], places)], axis=-1
    ).astype(jnp.bfloat16)
    q_nope = query[..., :QK_NOPE]
    q_rope = query[..., QK_NOPE:]
    latent = jnp.concatenate(
        [
            rms_scale(kv_latent[:, :KV_RANK].astype(jnp.float32), kv_gain),
            rotate(kv_latent[:, KV_RANK:].astype(jnp.float32), places),
        ],
        axis=-1,
    ).astype(jnp.bfloat16)
    kept = token_flags(segment_ids, trace_limit)
    qseg = lax.dynamic_slice_in_dim(segment_ids, offset, rows, 0)
    scale = (QK_NOPE + QK_ROPE) ** (-0.5)
    start_state = (
        jnp.full((heads, rows), -1e30, jnp.float32),
        jnp.zeros((heads, rows), jnp.float32),
        jnp.zeros((heads, rows, V_DIM), jnp.float32),
    )
    piece = lax.all_gather(latent, "ctx", axis=0, tiled=True)
    count = piece.shape[0]
    key_places = jnp.arange(count, dtype=jnp.int32)
    visible = (
        (qseg[:, None] == segment_ids[None, :])
        & (key_places[None, :] <= places[:, None])
        & kept[None, :]
    )

    def attend(state):
        top, total, summed = state
        keyval = jnp.dot(piece[:, :KV_RANK], kv_up, preferred_element_type=jnp.float32).astype(
            jnp.bfloat16
        )
        keyval = keyval.reshape(count, heads, QK_NOPE + V_DIM)
        scores = jnp.einsum(
            "thd,khd->htk", q_nope, keyval[..., :QK_NOPE], preferred_element_type=jnp.float32
        )
        scores = scores + jnp.einsum(
            "thd,kd->htk", q_rope, piece[:, KV_RANK:], preferred_element_type=jnp.float32
        )
        masked = jnp.where(visible[None], scores * scale, -1e30)
        new_top = jnp.maximum(top, jnp.max(masked, axis=-1))
        weights = jnp.where(visible[None], jnp.exp(masked - new_top[..., None]), 0.0)
        total = jnp.sum(weights, axis=-1)
        update = jnp.einsum(
            "htk,khd->htd",
            weights.astype(jnp.bfloat16),
            keyval[..., QK_NOPE:],
            preferred_element_type=jnp.float32,
        )
        return (new_top, total, update)

    top, total, summed = lax.cond(jnp.any(visible), attend, keep_state, start_state)
    attended = (
        jnp.transpose(summed / total[..., None], (1, 0, 2))
        .reshape(rows, heads * V_DIM)
        .astype(jnp.bfloat16)
    )
    partial_sum = jnp.dot(
        attended,
        lax.all_gather(out_proj, "ctx", axis=0, tiled=True),
        preferred_element_type=jnp.float32,
    )
    mixed = lax.psum_scatter(
        partial_sum.astype(jnp.bfloat16), "head", scatter_dimension=1, tiled=True
    )
    return mixed


def solution(mesh):
    in_specs = (
        P("ctx", None),
        P("ctx", None),
        P(),
        P(),
        P(None, "head"),
        P(None, "head"),
        P(("head", "ctx"), None),
        P(),
        P(),
    )
    out_specs = P("ctx", "head")
    return jax.shard_map(body, mesh=mesh, in_specs=in_specs, out_specs=out_specs, check_vma=False)
```

profile of v0, /device:TPU:65, one launch (start us, length us, event | category | flops | bytes accessed | tf_op | source)
XLA Modules:
  0.0 272.8 jit_solution(3691895455950281293)
XLA Ops:
  6.5 0.0 all-gather.3.cloned.1.call-start
  6.5 0.7 slice_convert_fusion.1
  7.3 1.0 fusion.27
  8.3 1.1 fusion.29
  9.3 0.1 multiply_cosine_fusion
  9.5 0.7 pad_maximum_fusion.1
  10.2 0.0 all-gather.3.cloned.1.call-update
  10.2 0.0 all-gather.5.cloned.1.call-start
  10.2 0.7 all-gather.5.cloned.1.call-update
  10.9 0.0 reduce-scatter.4.cloned.1.call-start
  11.0 1.2 fusion.20
  12.2 4.5 %fusion.23 = f32[128,1536]{0,1:T(8,128)S(1)} fusion(bf16[1536,1536]{1,0:T(8,128)(2,1)} %param.15, bf16[128,1536]{1,0:T(8,128)(2,1)} %param.11, f32[1536]{0:T(1024)} %param.13, f32[128]{0:T(128)S(1)} %add_rsqrt_fusion), kind=kOutput, calls=%fused_computation.32 | convolution fusion | flops 604766208 | bytes 5904896 | tf_op jit(solution)/shard_map/dot_general | solution.py:55
  16.7 0.8 dynamic_slice.3
  17.4 0.9 convert_reduce_fusion
  18.3 0.9 select_reduce_fusion.1
  19.2 3.2 %fusion.31 = (pred[]{:T(512)}, pred[128,4096]{0,1:T(8,128)(4,1)S(1)}) fusion(pred[4096]{0:T(1024)(128)(4,1)S(1)} %subtract_compare_fusion, s32[128]{0:T(128)S(1)} %get-tuple-element.53, s32[4096]{0:T(1024)} %param.18, s32[128]{0:T(128)S(1)} %dynamic_slice.3), kind=kLoop, calls=%fused_computation.60 | loop fusion | flops 2621439 | bytes 545793 | tf_op jit(solution)/shard_map/reduce_or | solution.py:111
  23.1 63.4 %all-gather.3.cloned.1.call-done = bf16[4096,576]{0,1:T(8,128)(2,1)} async-done(((bf16[128,576]{0,1:T(8,128)(2,1)}), bf16[4096,576]{0,1:T(8,128)(2,1)}) %all-gather.3.cloned.1.call-update) | async-done | bytes 4718608 | tf_op jit(solution)/shard_map/all_gather | solution.py:78
  86.5 59.7 %conditional.1 = (f32[8,128]{1,0:T(8,128)S(1)}, f32[8,128,128]{1,2,0:T(8,128)S(1)}) conditional(s32[]{:T(128)} %convert_element_type.48, () %tuple.13, (pred[128,4096]{0,1:T(8,128)(4,1)S(1)}, bf16[4096,576]{0,1:T(8,128)(2,1)}, bf16[512,2048]{1,0:T(8,128)(2,1)}, bf16[128,8,192]{0,2,1:T(8,128)(2,1)S(1)}) %tuple.14), branch_computations={%region_6.0_spmd, %region_7.10_spmd} | conditional | flops 11324619776 | bytes 127557648 | solution.py:111
  86.5 14.8 %convolution_convert_fusion = bf16[4096,2048]{0,1:T(8,128)(2,1)} fusion(bf16[512,2048]{1,0:T(8,128)(2,1)} %get-tuple-element.25, bf16[4096,576]{0,1:T(8,128)(2,1)} %get-tuple-element.17), kind=kOutput, calls=%fused_computation.4 | convolution fusion | flops 8598323200 | bytes 23068672 | tf_op jit(solution)/shard_map/cond/branch_1_fun/dot_general | solution.py:89
  101.4 0.2 copy.39
  101.6 12.0 %fusion.7 = f32[8,4096,128]{2,1,0:T(8,128)} fusion(bf16[4096,8,256]{0,2,1:T(8,128)(2,1)} %bitcast.25, bf16[128,8,192]{2,0,1:T(8,128)(2,1)S(1)} %copy.39), kind=kOutput, calls=%fused_computation.9 | convolution fusion | flops 1073741824 | bytes 25427968 | tf_op jit(solution)/shard_map/cond/branch_1_fun/thd,khd->htk/dot_general | solution.py:93
  113.6 11.2 %fusion.33 = (f32[8,128]{1,0:T(8,128)S(1)}, f32[8,128,4096]{1,2,0:T(8,128)}) fusion(bf16[128,8,192]{0,2,1:T(8,128)(2,1)S(1)} %get-tuple-element.37, bf16[4096,576]{0,1:T(8,128)(2,1)} %get-tuple-element.17, f32[8,4096,128]{2,1,0:T(8,128)} %fusion.7, pred[128,4096]{0,1:T(8,128)(4,1)S(1)} %get-tuple-element.16), kind=kOutput, calls=%fused_computation.61 | convolution fusion | flops 553647104 | bytes 34738176 | tf_op jit(solution)/shard_map/cond/branch_1_fun/thd,kd->htk/dot_general | solution.py:96
  124.9 12.2 %fusion.4 = f32[8,128,128]{1,2,0:T(8,128)S(1)} fusion(f32[8,128,4096]{1,2,0:T(8,128)} %get-tuple-element.44, bf16[4096,8,256]{0,2,1:T(8,128)(2,1)} %bitcast.26, f32[8,128]{1,0:T(8,128)S(1)} %broadcast_maximum_fusion, pred[128,4096]{0,1:T(8,128)(4,1)S(1)} %get-tuple-element.16), kind=kOutput, calls=%fused_computation.7 | convolution fusion | flops 1086324736 | bytes 26218496 | tf_op jit(solution)/shard_map/cond | solution.py:111
  137.1 9.0 %fusion.3 = f32[8,128]{1,0:T(8,128)S(1)} fusion(f32[8,128,4096]{1,2,0:T(8,128)} %get-tuple-element.44, f32[8,128]{1,0:T(8,128)S(1)} %broadcast_maximum_fusion, pred[128,4096]{0,1:T(8,128)(4,1)S(1)} %get-tuple-element.16), kind=kLoop, calls=%fused_computation.6 | loop fusion | flops 12581888 | bytes 17309696 | tf_op jit(solution)/shard_map/cond/branch_1_fun/reduce_sum | solution.py:102
  146.3 0.1 divide_convert_fusion
  146.3 31.1 %all-gather.5.cloned.1.call-done = bf16[1024,7168]{1,0:T(8,128)(2,1)} async-done(((bf16[32,7168]{1,0:T(8,128)(2,1)}), bf16[1024,7168]{1,0:T(8,128)(2,1)}) %all-gather.5.cloned.1.call-update) | async-done | bytes 14680080 | tf_op jit(solution)/shard_map/all_gather | solution.py:119
  177.4 7.3 %convolution_convert_fusion.1 = bf16[128,7168]{1,0:T(8,128)(2,1)S(1)} fusion(bf16[128,1024]{0,1:T(8,128)(2,1)S(1)} %bitcast.29, bf16[1024,7168]{1,0:T(8,128)(2,1)} %all-gather.5.cloned.1.call-done), kind=kOutput, calls=%fused_computation.21 | convolution fusion | flops 1879965696 | bytes 16777216 | tf_op jit(solution)/shard_map/dot_general | solution.py:117
  184.7 2.3 copy.43
  187.1 0.0 reduce-scatter.4.cloned.1.call-update
  187.1 77.4 %reduce-scatter.4.cloned.1.call-done = bf16[896,128]{1,0:T(8,128)(2,1)} async-done(((bf16[7168,128]{1,0:T(8,128)(2,1)}), bf16[896,128]{1,0:T(8,128)(2,1)}) %reduce-scatter.4.cloned.1.call-update) | async-done | bytes 229392
  264.5 1.8 copy.44
  (9 shorter events, 0.1 us)
Async XLA Ops:
  6.5 80.0 %all-gather.3.cloned.1.call-start = ((), (), s32[]{:S(2)}) async-start(), calls=%async_computation.1 | async-start | bytes 4866048 | tf_op jit(solution)/shard_map/all_gather | solution.py:78
  10.2 167.2 %all-gather.5.cloned.1.call-start = ((), (), s32[]{:S(2)}) async-start(), calls=%async_computation.2 | async-start | bytes 15138816 | tf_op jit(solution)/shard_map/all_gather | solution.py:119
  10.9 253.6 %reduce-scatter.4.cloned.1.call-start = ((), (), s32[]{:S(2)}) async-start(), calls=%async_computation.3 | async-start | bytes 2064384
Sparse Core Ops, SparseCore 0:
  10.3 76.1 all-gather.2
  88.4 88.9 all-gather.4
  187.2 77.2 reduce-scatter.3
where the time goes:
time: 275 us; the launch traced here: 273 us
  waiting for transfers between devices  173 us (63%)
  matrix products  62.1 us (23%)
  other arithmetic  18.7 us (7%)
  between operations  13.9 us (5%)
  local copies, waits for them, and re-layouts  5.11 us (2%)
    unnamed x4, waiting for transfers between devices  78.2 us
    all_gather x1, waiting for transfers between devices, body(): piece = lax.all_gather(latent, 'ctx', axis=0, tiled=True)  63.4 us
    all_gather x1, waiting for transfers between devices, body(): lax.all_gather(out_proj, 'ctx', axis=0, tiled=True)  31.1 us
    dot_general x1, matrix products, attend(): jnp.dot(piece[:, :KV_RANK], kv_up, preferred_element_type=jnp.float32)  14.8 us
    cond x1, matrix products, body(): lax.cond(jnp.any(visible), attend, keep_state, start_state)  12.2 us
    dot_general x1, matrix products, attend(): jnp.einsum('thd,khd->htk', q_nope, keyval[..., :QK_NOPE], preferred_eleme...  12 us
    dot_general x1, matrix products, attend(): jnp.einsum('thd,kd->htk', q_rope, piece[:, KV_RANK:], preferred_element_t...  11.2 us
    reduce_sum x1, other arithmetic, attend(): total = jnp.sum(weights, axis=-1)  8.95 us
  transfers between devices with their start and end apart: 3, of which 3 were waited for; matrix products, arithmetic and copies ran while one was open for 26% of the time, Pallas kernels for 0%

commit v1 on v0

v1 whole, which is shorter than its diff:
```python
import functools

import jax
import jax.numpy as jnp
import numpy as np
from jax import lax
from jax.experimental import pallas as pl
from jax.experimental.pallas import tpu as pltpu
from jax.sharding import PartitionSpec as P

MESH = pl.DeviceIdType.MESH
F32, BF16 = jnp.float32, jnp.bfloat16

ROWS = 128
KV_RANK = 512
NOPE = 128
ROPE = 64
HEADS = 8
Q_RANK = 1536
WINDOW = 9 * ROWS
LAT = KV_RANK + 128
BLOCK = 896
WIDTHS = (512, 384)
OFFS = (0, 512)
SCALE2 = float((NOPE + ROPE) ** (-0.5) * np.log2(np.e))


def tables():
    inverse = 10000.0 ** (-np.arange(32, dtype=np.float64) / 32)
    start = 128.0 * np.arange(32)[:, None] * inverse[None, :]
    step = 1.0 * np.arange(128)[:, None] * inverse[None, :]

    def both(angles):
        return np.concatenate([np.tile(np.cos(angles), 4), np.tile(np.sin(angles), 4)], 1).astype(np.float32)

    return both(start), both(step)


def kernel(
    q_latent, kv_latent, q_gain, kv_gain, q_up, kv_up, out_proj, seg, limit, start_tab, step_tab,
    out,
    ql_v, kvl_v, qg_v, kvg_v, qup_v, kvup_v, seg_v, start_v, step_v,
    lat, bias, query, att, w0, w1, p0, p1, ra0, ra1, rm0, rm1, acc, x0, x1, rx0, rx1,
    load_sem, own_sem, p1_send, p1_recv, ring_send, ring_recv, lat_send, lat_recv,
    att_send, att_recv, ra_send, ra_recv, rm_send, rm_recv, rx_send, rx_recv,
):
    ctx = lax.axis_index("ctx")
    head = lax.axis_index("head")
    z, i = ctx // 4, ctx % 4
    xl, c = i // 2, i % 2
    y, xh = head // 2, head % 2
    wbuf, pbuf, rabuf, rmbuf, xbuf, rxbuf = (w0, w1), (p0, p1), (ra0, ra1), (rm0, rm1), (x0, x1), (rx0, rx1)

    def at_z(step):
        return (((z + step + 8) % 8) * 4 + i, head)

    def at_mate(j):
        return (z * 4 + j, head)

    def at_y(step):
        return (ctx, ((y + step + 4) % 4) * 2 + xh)

    loads = []
    for n, (src, dst) in enumerate(
        ((kv_latent, kvl_v), (kv_gain, kvg_v), (start_tab, start_v), (step_tab, step_v), (seg, seg_v),
         (q_latent, ql_v), (q_gain, qg_v), (q_up, qup_v), (kv_up, kvup_v))
    ):
        copy = pltpu.make_async_copy(src, dst, load_sem.at[n])
        copy.start()
        loads.append(copy)

    def columns(hf, b, mate):
        block = 2 * (mate % 2 + 2 * b) + mate // 2
        return pl.ds(pl.multiple_of(block * BLOCK + OFFS[hf], 128), WIDTHS[hf])

    own_rows = pl.ds(pl.multiple_of(z * 128 + i * 32, 32), 32)

    barrier = pltpu.get_barrier_semaphore()

    def tell(device):
        pl.semaphore_signal(barrier, inc=1, device_id=device, device_id_type=MESH)

    even = (y + c) % 2 == 0
    for step in (-1, -2, 1):
        tell(at_z(step))
    for d in (1, 2, 3):
        tell(at_mate((i + d) % 4))
    for step in (-1, 1):
        tell(at_y(step))
    for other in (0, 1):
        source = 2 * xh + y % 2
        me = (other == xh) & (source == i)

        @pl.when(jnp.logical_not(me))
        def _():
            tell((z * 4 + source, 2 * y + other))

    for n in (0, 1, 2, 3):
        loads[n].wait()
    lane = lax.broadcasted_iota(jnp.int32, (1, 128), 1)
    a = start_v[pl.ds(ctx, 1), :]
    s = step_v[...]
    cos = a[:, :128] * s[:, :128] - a[:, 128:] * s[:, 128:]
    sin = a[:, 128:] * s[:, :128] + a[:, :128] * s[:, 128:]
    low = (lane % 64) < 32
    sin = jnp.where(low, -sin, sin)

    def rotate(v):
        swapped = jnp.where(low, pltpu.roll(v, 96, 1), pltpu.roll(v, 32, 1))
        return v * cos + swapped * sin

    own_lat = pl.ds(pl.multiple_of((8 + i) * 128, 128), 128)
    raw = kvl_v[:, :KV_RANK].astype(F32)
    normed = raw * lax.rsqrt(jnp.mean(raw * raw, axis=-1, keepdims=True) + 1e-06) * kvg_v[...]
    lat[own_lat, :KV_RANK] = normed.astype(BF16)
    kr = kvl_v[:, KV_RANK:].astype(F32)
    lat[own_lat, KV_RANK:] = rotate(jnp.concatenate([kr, kr], axis=1)).astype(BF16)

    pl.semaphore_wait(
        barrier, 8 + jnp.where(even, 4 - (xh == xl).astype(jnp.int32), 0)
    )

    spreads = {}

    def spread(hf, b):
        own = pltpu.make_async_copy(
            out_proj.at[:, columns(hf, b, i)], wbuf[hf].at[b, own_rows, :], own_sem.at[hf, b]
        )
        own.start()
        copies = [own]
        for d in (1, 2, 3):
            mate = (i + d) % 4
            copy = pltpu.make_async_remote_copy(
                src_ref=out_proj.at[:, columns(hf, b, mate)],
                dst_ref=wbuf[hf].at[b, own_rows, :],
                send_sem=p1_send.at[hf, b, d - 1],
                recv_sem=p1_recv.at[hf, b, d - 1],
                device_id=at_mate(mate),
                device_id_type=MESH,
            )
            copy.start()
            copies.append(copy)
        spreads[hf, b] = copies

    def send_latent(n, slot, device):
        rows = pl.ds(pl.multiple_of(slot * 128, 128), 128)
        return lat.at[rows, :], n, device

    def lat_copy(n, src_slot, dst_slot, device):
        src = pl.ds(pl.multiple_of(src_slot * 128, 128), 128)
        dst = pl.ds(pl.multiple_of(dst_slot * 128, 128), 128)
        return pltpu.make_async_remote_copy(
            src_ref=lat.at[src, :], dst_ref=lat.at[dst, :],
            send_sem=lat_send.at[n], recv_sem=lat_recv.at[n],
            device_id=device, device_id_type=MESH,
        )

    ring = {}

    def ring_start(hf, b, way, step):
        shift = -(step - 1) if way == 0 else step - 1
        block = (z + shift + 8) % 8
        rows = pl.ds(pl.multiple_of(block * 128, 128), 128)
        copy = pltpu.make_async_remote_copy(
            src_ref=wbuf[hf].at[b, rows, :], dst_ref=wbuf[hf].at[b, rows, :],
            send_sem=ring_send.at[hf, b, way, step - 1], recv_sem=ring_recv.at[hf, b, way, step - 1],
            device_id=at_z(1 if way == 0 else -1), device_id_type=MESH,
        )
        copy.start()
        ring[hf, b, way, step] = copy

    def ring_event(hf, b, step):
        if step == 1:
            for n, copy in enumerate(spreads[hf, b]):
                if n == 0:
                    copy.wait()
                else:
                    copy.wait_recv()
        for way, last in ((1, 4), (0, 3)):
            if 1 < step <= last + 1:
                ring[hf, b, way, step - 1].wait_recv()
            if step <= last:
                ring_start(hf, b, way, step)

    spread(0, 0)
    one = lat_copy(0, 8 + i, 4 + i, at_z(1))
    two = lat_copy(1, 8 + i, i, at_z(2))
    one.start()
    two.start()
    for d in (1, 2, 3):
        @pl.when(i + d < 4)
        def _():
            lat_copy(1 + d, 8 + i, 8 + i, at_mate(i + d)).start()
    spread(0, 1)

    loads[4].wait()
    everything = seg_v[...]
    starts = []
    for t in range(8):
        below = (everything < t).astype(F32)
        starts.append(jnp.sum(jnp.sum(below, axis=0, keepdims=True), axis=1, keepdims=True).astype(jnp.int32))
    row = lax.broadcasted_iota(jnp.int32, (128, 128), 0)
    column = lax.broadcasted_iota(jnp.int32, (128, 128), 1)
    mine = seg_v[pl.ds(ctx, 1), :]
    qseg = jnp.sum(jnp.where(row == column, mine.astype(F32), 0.0), axis=1, keepdims=True).astype(jnp.int32)
    qplace = ctx * 128 + lax.broadcasted_iota(jnp.int32, (128, 1), 0)
    for n in range(9):
        block = (ctx + 24 + n) % 32
        kseg = seg_v[pl.ds(block, 1), :]
        kplace = block * 128 + lane
        room = jnp.zeros((1, 128), jnp.int32)
        for t in range(8):
            room = room + jnp.where(kseg == t, starts[t] + limit[t], 0)
        kplace_kept = jnp.where(kplace < room, kplace, 1 << 20)
        visible = (qseg == kseg) & (kplace_kept <= qplace)
        bias[:, n * 128:(n + 1) * 128] = jnp.where(visible, 0.0, -1e30)

    ring_event(0, 0, 1)

    one.wait_recv()
    passed = []
    for d in (1, 2, 3):
        copy = lat_copy(4 + d, 4 + i, 4 + i, at_mate((i + d) % 4))
        copy.start()
        passed.append(copy)
    ring_event(0, 1, 1)

    loads[5].wait()
    loads[6].wait()
    raw = ql_v[...].astype(F32)
    qnorm = (raw * lax.rsqrt(jnp.mean(raw * raw, axis=-1, keepdims=True) + 1e-06) * qg_v[...]).astype(BF16)
    two.wait_recv()
    for d in (1, 2, 3):
        @pl.when(i - d >= 0)
        def _():
            lat_copy(7 + d, i, i, at_mate(i - d)).start()
    loads[7].wait()
    half = lane < 64
    for g in range(4):
        three = jnp.dot(qnorm, qup_v[:, g * 384:(g + 1) * 384], preferred_element_type=F32)
        t0, t1, t2 = three[:, :128], three[:, 128:256], three[:, 256:]
        second = jnp.where(half, pltpu.roll(t1, 64, 1), pltpu.roll(t2, 64, 1))
        turned = rotate(jnp.where(half, t1, t2))
        query[2 * g, :, :128] = t0.astype(BF16)
        query[2 * g, :, 128:] = jnp.where(half, turned, 0.0).astype(BF16)
        query[2 * g + 1, :, :128] = second.astype(BF16)
        query[2 * g + 1, :, 128:] = jnp.where(half, 0.0, turned).astype(BF16)

    ring_event(0, 0, 2)
    spread(1, 0)
    ring_event(0, 1, 2)
    spread(1, 1)

    for d in (1, 2, 3):
        @pl.when(i - d >= 0)
        def _():
            lat_copy(1 + d, 8 + i, 8 + i, at_mate(i)).wait_recv()
        passed[d - 1].wait_recv()

        @pl.when(i + d < 4)
        def _():
            lat_copy(7 + d, i, i, at_mate(i)).wait_recv()
    loads[8].wait()
    ring_event(0, 0, 3)

    win = pl.ds(pl.multiple_of(i * 128, 128), WINDOW)
    own_att = pl.ds(pl.multiple_of(i * 128, 128), 128)
    att_copies = []

    def one_head(h):
        keyval = jnp.dot(
            lat[win, :KV_RANK], kvup_v[:, h * 256:(h + 1) * 256], preferred_element_type=F32
        ).astype(BF16)
        keys = jnp.concatenate([keyval[:, :128], lat[win, KV_RANK:]], axis=1)
        scores = lax.dot_general(query[h], keys, (((1,), (1,)), ((), ())), preferred_element_type=F32)
        masked = scores * SCALE2 + bias[...]
        weights = jnp.exp2(masked - jnp.max(masked, axis=1, keepdims=True))
        total = jnp.sum(weights, axis=1, keepdims=True)
        summed = jnp.dot(weights.astype(BF16), keyval[:, 128:], preferred_element_type=F32)
        att[own_att, h * 128:(h + 1) * 128] = (summed / total).astype(BF16)

    events = {1: (0, 1, 3), 2: (0, 0, 4), 3: (1, 0, 1), 4: (0, 1, 4), 5: (1, 1, 1), 7: (1, 0, 2)}
    for h in range(8):
        one_head(h)
        if h % 2 == 1:
            g = h // 2
            for d in (1, 2, 3):
                part = att.at[own_att, g * 256:(g + 1) * 256]
                copy = pltpu.make_async_remote_copy(
                    src_ref=part, dst_ref=part, send_sem=att_send.at[g, d - 1], recv_sem=att_recv.at[g, d - 1],
                    device_id=at_mate((i + d) % 4), device_id_type=MESH,
                )
                copy.start()
                att_copies.append(copy)
        if h in events:
            ring_event(*events[h])

    def partial(hf, b):
        return jnp.dot(att[...], wbuf[hf][b], preferred_element_type=F32)

    def ra_copy(hf, side):
        return pltpu.make_async_remote_copy(
            src_ref=pbuf[hf].at[0, side * 256:(side + 1) * 256, :], dst_ref=rabuf[hf].at[side],
            send_sem=ra_send.at[hf, side], recv_sem=ra_recv.at[hf, side],
            device_id=at_y(1 - 2 * side), device_id_type=MESH,
        )

    def rm_copy(hf, side):
        return pltpu.make_async_remote_copy(
            src_ref=pbuf[hf].at[side], dst_ref=rmbuf[hf].at[side],
            send_sem=rm_send.at[hf, side], recv_sem=rm_recv.at[hf, side],
            device_id=at_y(1 - 2 * side), device_id_type=MESH,
        )

    def rx_pieces(hf, j):
        src = xbuf[hf].at[j * 128:(j + 1) * 128, :]
        dst = rxbuf[hf].at[xh]
        self_copy = pltpu.make_async_copy(src, dst, rx_recv.at[hf, xh])
        far_copy = pltpu.make_async_remote_copy(
            src_ref=src, dst_ref=dst, send_sem=rx_send.at[hf, j], recv_sem=rx_recv.at[hf, xh],
            device_id=(z * 4 + j, 2 * y + xl), device_id_type=MESH,
        )
        return self_copy, far_copy, (xh == xl) & (i == j)

    def reduce_first(hf):
        w = WIDTHS[hf]
        toward_next = ((y + 1 - c + 4) % 4) // 2
        own = ((y - c + 4) % 4) // 2

        @pl.when(even)
        def _():
            pbuf[hf][0] = partial(hf, 1 - own).astype(BF16)
            ra_copy(hf, 0).start()
            ra_copy(hf, 1).start()
            acc[:, :w] = partial(hf, own)

        @pl.when(jnp.logical_not(even))
        def _():
            for side, b in ((0, toward_next), (1, 1 - toward_next)):
                acc[:, :w] = partial(hf, b)
                ra_copy(hf, side).wait_recv()
                here = slice(side * 256, (side + 1) * 256)
                there = slice((1 - side) * 256, (2 - side) * 256)
                pbuf[hf][side, here, :] = (acc[here, :w] + rabuf[hf][side].astype(F32)).astype(BF16)
                pbuf[hf][side, there, :] = acc[there, :w].astype(BF16)
                rm_copy(hf, side).start()

    def reduce_second(hf):
        w = WIDTHS[hf]

        @pl.when(even)
        def _():
            rm_copy(hf, 0).wait_recv()
            rm_copy(hf, 1).wait_recv()
            xbuf[hf][...] = (
                acc[:, :w] + rmbuf[hf][0].astype(F32) + rmbuf[hf][1].astype(F32)
            ).astype(BF16)
            for j in range(4):
                self_copy, far_copy, me = rx_pieces(hf, j)

                @pl.when(me)
                def _():
                    self_copy.start()

                @pl.when(jnp.logical_not(me))
                def _():
                    far_copy.start()

    def reduce_last(hf):
        w = WIDTHS[hf]
        for n in range(2):
            pltpu.make_async_copy(rxbuf[hf].at[n], rxbuf[hf].at[n], rx_recv.at[hf, n]).wait()
        out[:, OFFS[hf]:OFFS[hf] + w] = (rxbuf[hf][0].astype(F32) + rxbuf[hf][1].astype(F32)).astype(BF16)

    for copy in att_copies:
        copy.wait_recv()
    ring_event(0, 0, 5)
    ring_event(1, 1, 2)
    ring_event(0, 1, 5)
    reduce_first(0)
    ring_event(1, 0, 3)
    ring_event(1, 1, 3)
    reduce_second(0)
    ring_event(1, 0, 4)
    ring_event(1, 1, 4)
    reduce_last(0)
    ring_event(1, 0, 5)
    ring_event(1, 1, 5)
    reduce_first(1)
    reduce_second(1)
    reduce_last(1)

    for copies in spreads.values():
        for copy in copies[1:]:
            copy.wait_send()
    for copy in ring.values():
        copy.wait_send()
    for copy in (one, two, *passed, *att_copies):
        copy.wait_send()
    for d in (1, 2, 3):
        @pl.when(i + d < 4)
        def _():
            lat_copy(1 + d, 8 + i, 8 + i, at_mate(i)).wait_send()

        @pl.when(i - d >= 0)
        def _():
            lat_copy(7 + d, i, i, at_mate(i)).wait_send()

    @pl.when(even)
    def _():
        for hf in (0, 1):
            ra_copy(hf, 0).wait_send()
            ra_copy(hf, 1).wait_send()
            for j in range(4):
                _, far_copy, me = rx_pieces(hf, j)

                @pl.when(jnp.logical_not(me))
                def _():
                    far_copy.wait_send()

    @pl.when(jnp.logical_not(even))
    def _():
        for hf in (0, 1):
            rm_copy(hf, 0).wait_send()
            rm_copy(hf, 1).wait_send()


def body(q_latent, kv_latent, q_gain, kv_gain, q_up, kv_up, out_proj, segment_ids, trace_limit):
    start_tab, step_tab = tables()
    any_spec = pl.BlockSpec(memory_space=pl.ANY)
    dma = pltpu.SemaphoreType.DMA
    wa, wb = WIDTHS
    scratch = [
        pltpu.VMEM((ROWS, Q_RANK), BF16),
        pltpu.VMEM((ROWS, KV_RANK + ROPE), BF16),
        pltpu.VMEM((1, Q_RANK), F32),
        pltpu.VMEM((1, KV_RANK), F32),
        pltpu.VMEM((Q_RANK, HEADS * (NOPE + ROPE)), BF16),
        pltpu.VMEM((KV_RANK, HEADS * 256), BF16),
        pltpu.VMEM((32, 128), jnp.int32),
        pltpu.VMEM((32, 256), F32),
        pltpu.VMEM((128, 256), F32),
        pltpu.VMEM((12 * ROWS, LAT), BF16),
        pltpu.VMEM((ROWS, WINDOW), F32),
        pltpu.VMEM((HEADS, ROWS, 256), BF16),
        pltpu.VMEM((4 * ROWS, HEADS * 128), BF16),
        pltpu.VMEM((2, 1024, wa), BF16),
        pltpu.VMEM((2, 1024, wb), BF16),
        pltpu.VMEM((2, 512, wa), BF16),
        pltpu.VMEM((2, 512, wb), BF16),
        pltpu.VMEM((2, 256, wa), BF16),
        pltpu.VMEM((2, 256, wb), BF16),
        pltpu.VMEM((2, 512, wa), BF16),
        pltpu.VMEM((2, 512, wb), BF16),
        pltpu.VMEM((512, wa), F32),
        pltpu.VMEM((512, wa), BF16),
        pltpu.VMEM((512, wb), BF16),
        pltpu.VMEM((2, ROWS, wa), BF16),
        pltpu.VMEM((2, ROWS, wb), BF16),
        dma((9,)),
        dma((2, 2)),
        dma((2, 2, 3)),
        dma((2, 2, 3)),
        dma((2, 2, 2, 4)),
        dma((2, 2, 2, 4)),
        dma((11,)),
        dma((11,)),
        dma((4, 3)),
        dma((4, 3)),
        dma((2, 2)),
        dma((2, 2)),
        dma((2, 2)),
        dma((2, 2)),
        dma((2, 4)),
        dma((2, 2)),
    ]
    return pl.pallas_call(
        kernel,
        out_shape=jax.ShapeDtypeStruct((ROWS, BLOCK), BF16),
        in_specs=[any_spec] * 8 + [pl.BlockSpec(memory_space=pltpu.SMEM)] + [any_spec] * 2,
        out_specs=pl.BlockSpec(memory_space=pltpu.VMEM),
        scratch_shapes=scratch,
        compiler_params=pltpu.CompilerParams(
            collective_id=0, has_side_effects=True, vmem_limit_bytes=56 * 2**20
        ),
        name="latent_attention",
    )(
        q_latent, kv_latent, q_gain.reshape(1, Q_RANK), kv_gain.reshape(1, KV_RANK), q_up, kv_up, out_proj,
        segment_ids.reshape(32, 128), trace_limit, jnp.asarray(start_tab), jnp.asarray(step_tab),
    )


def solution(mesh):
    in_specs = (
        P("ctx", None),
        P("ctx", None),
        P(),
        P(),
        P(None, "head"),
        P(None, "head"),
        P(("head", "ctx"), None),
        P(),
        P(),
    )
    return jax.shard_map(body, mesh=mesh, in_specs=in_specs, out_specs=P("ctx", "head"), check_vma=False)
```

time: 275 us -> 97.1 us (0.35)
  waiting for transfers between devices: 173 us -> 0 us
  Pallas kernels: 0 us -> 92.1 us
  matrix products: 62.1 us -> 0 us
  other arithmetic: 18.7 us -> 0 us
  between operations: 13.9 us -> 0.01 us
    all_gather x2 -> x0, waiting for transfers between devices: 94.5 us -> none  [the longest x1 63.4 us: body(): piece = lax.all_gather(latent, 'ctx', axis=0, tiled=True)]
    pallas_call x0 -> x1, Pallas kernels: none -> 92.1 us  [body(): pl.pallas_call(kernel, out_shape=jax.ShapeDtypeStruct((ROWS, BLOCK), BF16...]
    unnamed x4 -> x0, waiting for transfers between devices: 78.2 us -> none
    dot_general x5 -> x0, matrix products: 49.9 us -> none  [the longest x1 14.8 us: attend(): jnp.dot(piece[:, :KV_RANK], kv_up, preferred_element_type=jnp.float32)]
    reduce_sum x5 -> x0, other arithmetic: 12.8 us -> none  [the longest x1 8.95 us: attend(): total = jnp.sum(weights, axis=-1)]
    cond x1 -> x0, matrix products: 12.2 us -> none  [body(): lax.cond(jnp.any(visible), attend, keep_state, start_state)]
    reduce_or x1 -> x0, other arithmetic: 3.15 us -> none  [body(): jnp.any(visible)]
  transfers between devices with their start and end apart: 3 -> 0, of which waited for: 3 -> 0; matrix products, arithmetic and copies ran while one was open for 26% -> 0% of each run, Pallas kernels for 0% -> 0%
where the time goes in v1:
time: 97.1 us; the launch traced here: 96.8 us
  Pallas kernels  92.1 us (95%)
  local copies, waits for them, and re-layouts  4.65 us (5%)
    pallas_call x1, Pallas kernels, body(): pl.pallas_call(kernel, out_shape=jax.ShapeDtypeStruct((ROWS, BLOCK), BF16...  92.1 us
    unnamed x2, local copies, waits for them, and re-layouts  3.36 us

profile of v1, /device:TPU:65, one launch (start us, length us, event | category | flops | bytes accessed | tf_op | source)
XLA Modules:
  0.0 96.8 jit_solution(14702678565322051329)
XLA Ops:
  0.0 1.3 %reshape.9.q_gain = f32[1,1536]{1,0:T(1,128)} reshape(f32[1536]{0:T(1024)} %param.13) | data formatting | bytes 12288 | tf_op jit(solution)/shard_map/reshape | solution.py:488
  1.3 1.7 %copy.12.kv_latent = bf16[128,576]{1,0:T(8,128)(2,1)} copy(bf16[128,576]{0,1:T(8,128)(2,1)} %param.12) | data formatting | bytes 294912 | tf_op args[1]
  3.0 92.1 %latent_attention.1 = bf16[128,896]{1,0:T(8,128)(2,1)} custom-call(bf16[128,1536]{1,0:T(8,128)(2,1)} %q_latent.1, bf16[128,576]{1,0:T(8,128)(2,1)} %copy.12.kv_latent, f32[1,1536]{1,0:T(1,128)} %reshape.9.q_gain, f32[1,512]{1,0:T(1,128)} %bitcast.3, bf16[1536,1536]{1,0:T(8,128)(2,1)} %q_up.1, bf16[512,2048]{1,0:T(8,128)(2,1)} %kv_up.1, ...), custom_call_target="tpu_custom_call" | custom-call | tf_op jit(solution)/shard_map/latent_attention/pallas_call | solution.py:477
  95.2 1.6 %copy.14 = bf16[128,896]{1,0:T(8,128)(2,1)} copy(bf16[128,896]{1,0:T(8,128)(2,1)} %latent_attention.1) | data formatting | bytes 458752

commit v2 on v0

v2 whole, which is shorter than its diff:
```python
import functools

import jax
import jax.numpy as jnp
import numpy as np
from jax import lax
from jax.experimental import pallas as pl
from jax.experimental.pallas import tpu as pltpu
from jax.sharding import PartitionSpec as P

MESH = pl.DeviceIdType.MESH
F32, BF16 = jnp.float32, jnp.bfloat16

ROWS = 128
KV_RANK = 512
NOPE = 128
ROPE = 64
HEADS = 8
Q_RANK = 1536
WINDOW = 9 * ROWS
LAT = KV_RANK + 128
BLOCK = 896
WIDTHS = (128, 256, 256, 128, 128)
OFFS = (0, 128, 384, 640, 768)
PARTS = len(WIDTHS)
SCALE2 = float((NOPE + ROPE) ** (-0.5) * np.log2(np.e))


def tables():
    inverse = 10000.0 ** (-np.arange(32, dtype=np.float64) / 32)
    start = 128.0 * np.arange(32)[:, None] * inverse[None, :]
    step = 1.0 * np.arange(128)[:, None] * inverse[None, :]

    def both(angles):
        return np.concatenate([np.tile(np.cos(angles), 4), np.tile(np.sin(angles), 4)], 1).astype(np.float32)

    return both(start), both(step)


def kernel(
    q_latent, kv_latent, q_gain, kv_gain, q_up, kv_up, out_proj, seg, limit, start_tab, step_tab,
    out,
    ql_v, kvl_v, qg_v, kvg_v, qup_v, kvup_v, seg_v, start_v, step_v, lat, keyval, bias, query, att, final,
    wbuf, pbuf, rabuf, rmbuf, acc,
    load_sem, own_sem, spread_send, spread_recv, ring_send, ring_recv, lat_send, lat_recv,
    att_send, att_recv, ra_send, ra_recv, rm_send, rm_recv, rx_send, rx_recv,
):
    ctx = lax.axis_index("ctx")
    head = lax.axis_index("head")
    z, i = ctx // 4, ctx % 4
    xl, c = i // 2, i % 2
    y, xh = head // 2, head % 2
    x = 2 * xh + xl

    def at_z(step):
        return (((z + step + 8) % 8) * 4 + i, head)

    def at_x(there, core):
        return (z * 4 + (there % 2) * 2 + core, y * 2 + there // 2)

    def at_y(step):
        return (ctx, ((y + step + 4) % 4) * 2 + xh)

    sent = []

    def send(src, dst, send_sem, recv_sem, device):
        copy = pltpu.make_async_remote_copy(
            src_ref=src, dst_ref=dst, send_sem=send_sem, recv_sem=recv_sem, device_id=device, device_id_type=MESH
        )
        copy.start()
        sent.append(copy)
        return copy

    loads = []
    for n, (src, dst) in enumerate(
        ((kv_latent, kvl_v), (kv_gain, kvg_v), (start_tab, start_v), (step_tab, step_v), (seg, seg_v),
         (q_latent, ql_v), (q_gain, qg_v), (q_up, qup_v), (kv_up, kvup_v))
    ):
        copy = pltpu.make_async_copy(src, dst, load_sem.at[n])
        copy.start()
        loads.append(copy)

    barrier = pltpu.get_barrier_semaphore()

    def tell(device):
        pl.semaphore_signal(barrier, inc=1, device_id=device, device_id_type=MESH)

    for step in (-1, 1):
        tell(at_z(step))
        tell(at_y(step))
    place = x * 2 + c
    for d in range(1, 8):
        other = (place + d) % 8
        tell(at_x(other // 2, other % 2))

    for n in (0, 1, 2, 3):
        loads[n].wait()
    lane = lax.broadcasted_iota(jnp.int32, (1, 128), 1)
    a = start_v[pl.ds(ctx, 1), :]
    s = step_v[...]
    cos = a[:, :128] * s[:, :128] - a[:, 128:] * s[:, 128:]
    sin = a[:, 128:] * s[:, :128] + a[:, :128] * s[:, 128:]
    low = (lane % 64) < 32
    sin = jnp.where(low, -sin, sin)

    def rotate(v):
        swapped = jnp.where(low, pltpu.roll(v, 96, 1), pltpu.roll(v, 32, 1))
        return v * cos + swapped * sin

    def slot(p, j):
        return pl.ds(pl.multiple_of((p * 4 + j) * 128, 128), 128)

    raw = jnp.transpose(kvl_v[:KV_RANK, :].astype(F32))
    normed = raw * lax.rsqrt(jnp.mean(raw * raw, axis=-1, keepdims=True) + 1e-06) * kvg_v[...]
    lat[slot(2, i), :KV_RANK] = normed.astype(BF16)
    kr = kvl_v[KV_RANK:, :].astype(F32)
    lat[slot(2, i), KV_RANK:] = rotate(jnp.transpose(jnp.concatenate([kr, kr], axis=0))).astype(BF16)

    pl.semaphore_wait(barrier, 11)

    def lat_z(p):
        part_src, part_dst = lat.at[slot(p, i), :], lat.at[slot(p - 1, i), :]
        return send(part_src, part_dst, lat_send.at[p - 1, 0], lat_recv.at[p - 1, 0], at_z(1))

    def lat_spread(p):
        start = (p * 4 + i) * 128
        copies = []
        for n in (0, 1):
            part = lat.at[pl.ds(pl.multiple_of(start + n * 64, 64), 64), :]
            copies.append(
                send(part, part, lat_send.at[p, 1 + n], lat_recv.at[p, 1 + n], at_x((x + 1 + 2 * n) % 4, c))
            )
        part = lat.at[slot(p, i), :]
        copies.append(send(part, part, lat_send.at[p, 3], lat_recv.at[p, 3], at_x(x, 1 - c)))
        return copies

    def lat_pass(p, copies):
        copies[0].wait_recv()
        copies[1].wait_recv()
        part = lat.at[slot(p, 2 * (1 - xl) + c), :]
        copies.append(send(part, part, lat_send.at[p, 4], lat_recv.at[p, 4], at_x(x, 1 - c)))

    own_rows = pl.ds(pl.multiple_of(i * 32, 32), 32)
    spreads = {}

    def columns(k, there, core):
        block = 2 * (there % 2 + 2 * core) + there // 2
        return pl.ds(pl.multiple_of(block * BLOCK + OFFS[k], 128), WIDTHS[k])

    def spread(k):
        dst = wbuf[k].at[z, xh, own_rows, :]
        own = pltpu.make_async_copy(out_proj.at[:, columns(k, x, c)], dst, own_sem.at[k])
        own.start()
        copies = []
        for d in range(1, 8):
            other = (place + d) % 8
            there, core = other // 2, other % 2
            copies.append(
                send(out_proj.at[:, columns(k, there, core)], dst, spread_send.at[k, d - 1],
                     spread_recv.at[k, d - 1], at_x(there, core))
            )
        spreads[k] = (own, copies)

    ring = {}

    def ring_event(k, step, way):
        if step == 1 and way == 1:
            own, copies = spreads[k]
            own.wait()
            for copy in copies:
                copy.wait_recv()
        if step > 1:
            ring[k, way, step - 1].wait_recv()
        if step <= 3 + way:
            block = (z + (step - 1) * (2 * way - 1) + 8) % 8
            part = wbuf[k].at[block]
            ring[k, way, step] = send(
                part, part, ring_send.at[k, way, step - 1], ring_recv.at[k, way, step - 1], at_z(1 - 2 * way)
            )

    def plus(*events):
        for k, step in events:
            ring_event(k, step, 0)

    def minus(*events):
        for k, step in events:
            ring_event(k, step, 1)

    spread(0)
    lat_z(2)
    lat2 = lat_spread(2)
    spread(1)
    spread(2)
    spread(3)
    spread(4)

    loads[4].wait()
    everything = seg_v[...]
    starts = []
    for t in range(8):
        below = (everything < t).astype(F32)
        starts.append(jnp.sum(jnp.sum(below, axis=0, keepdims=True), axis=1, keepdims=True).astype(jnp.int32))
    row = lax.broadcasted_iota(jnp.int32, (128, 128), 0)
    column = lax.broadcasted_iota(jnp.int32, (128, 128), 1)
    mine = seg_v[pl.ds(ctx, 1), :]
    qseg = jnp.sum(jnp.where(row == column, mine.astype(F32), 0.0), axis=1, keepdims=True).astype(jnp.int32)
    qplace = ctx * 128 + lax.broadcasted_iota(jnp.int32, (128, 1), 0)
    for n in range(9):
        block = (ctx + 24 + n) % 32
        kseg = seg_v[pl.ds(block, 1), :]
        kplace = block * 128 + lane
        room = jnp.zeros((1, 128), jnp.int32)
        for t in range(8):
            room = room + jnp.where(kseg == t, starts[t] + limit[t], 0)
        kplace_kept = jnp.where(kplace < room, kplace, 1 << 20)
        visible = (qseg == kseg) & (kplace_kept <= qplace)
        bias[:, n * 128:(n + 1) * 128] = jnp.where(visible, 0.0, -1e30)

    minus((0, 1), (1, 1))
    lat_pass(2, lat2)
    lat_first = pltpu.make_async_remote_copy(
        src_ref=lat.at[slot(1, i), :], dst_ref=lat.at[slot(1, i), :], send_sem=lat_send.at[1, 0],
        recv_sem=lat_recv.at[1, 0], device_id=at_z(1), device_id_type=MESH,
    )
    lat_first.wait_recv()
    lat_second = lat_z(1)
    lat1 = lat_spread(1)
    minus((2, 1), (0, 2), (3, 1), (4, 1))

    loads[5].wait()
    loads[6].wait()
    raw = ql_v[...].astype(F32)
    q_gain_row = jnp.concatenate([qg_v[t:t + 1, :] for t in range(Q_RANK // 128)], axis=1)
    qnorm = (raw * lax.rsqrt(jnp.mean(raw * raw, axis=-1, keepdims=True) + 1e-06) * q_gain_row).astype(BF16)
    loads[7].wait()
    half = lane < 64

    def queries(g):
        three = jnp.dot(qnorm, qup_v[:, g * 384:(g + 1) * 384], preferred_element_type=F32)
        t0, t1, t2 = three[:, :128], three[:, 128:256], three[:, 256:]
        second = jnp.where(half, pltpu.roll(t1, 64, 1), pltpu.roll(t2, 64, 1))
        turned = rotate(jnp.where(half, t1, t2))
        query[2 * g, :, :128] = t0.astype(BF16)
        query[2 * g, :, 128:] = jnp.where(half, turned, 0.0).astype(BF16)
        query[2 * g + 1, :, :128] = second.astype(BF16)
        query[2 * g + 1, :, 128:] = jnp.where(half, 0.0, turned).astype(BF16)

    def project(p):
        for n in range(4):
            cols = slice(n * 512, (n + 1) * 512)
            keyval[p * 512:(p + 1) * 512, cols] = jnp.dot(
                lat[p * 512:(p + 1) * 512, :KV_RANK], kvup_v[:, cols], preferred_element_type=F32
            ).astype(BF16)

    for g in range(4):
        queries(g)
    minus((1, 2))
    lat_pass(1, lat1)
    loads[8].wait()
    lat2[2].wait_recv()
    lat2[3].wait_recv()
    project(2)
    lat_second.wait_recv()
    lat0 = lat_spread(0)
    plus((0, 1), (1, 1), (2, 1), (3, 1), (4, 1))
    minus((2, 2))
    lat1[2].wait_recv()
    lat1[3].wait_recv()
    project(1)
    lat_pass(0, lat0)
    minus((3, 2), (4, 2))
    plus((0, 2))
    lat0[2].wait_recv()
    lat0[3].wait_recv()
    project(0)

    win = pl.ds(pl.multiple_of(i * 128, 128), WINDOW)

    def one_head(h):
        keys = jnp.concatenate([keyval[win, h * 256:h * 256 + 128], lat[win, KV_RANK:]], axis=1)
        scores = lax.dot_general(query[h], keys, (((1,), (1,)), ((), ())), preferred_element_type=F32)
        masked = scores * SCALE2 + bias[...]
        weights = jnp.exp2(masked - jnp.max(masked, axis=1, keepdims=True))
        total = jnp.sum(weights, axis=1, keepdims=True)
        summed = jnp.dot(weights.astype(BF16), keyval[win, h * 256 + 128:(h + 1) * 256], preferred_element_type=F32)
        rows = pl.ds(pl.multiple_of(i * 128, 128), 128)
        att[xh, rows, h * 128:(h + 1) * 128] = (summed / total).astype(BF16)

    def att_part(g, there, first=0, count=128):
        begin = ((there % 2) * 2 + c) * 128 + first
        return att.at[there // 2, pl.ds(pl.multiple_of(begin, 64), count), g * 256:(g + 1) * 256]

    att1, att2 = {}, {}

    def att_send_own(g):
        part = att_part(g, x)
        att1[g] = [
            send(part, part, att_send.at[g, n], att_recv.at[g, n], at_x((x + 1 + n) % 4, c)) for n in range(3)
        ]
        att2[g] = [send(part, part, att_send.at[g, 3], att_recv.at[g, 3], at_x(x, 1 - c))]

    def att_pass(g):
        for n in (0, 2, 1):
            att1[g][n].wait_recv()
            part = att_part(g, (x + 3 - n) % 4)
            att2[g].append(send(part, part, att_send.at[g, 4 + n], att_recv.at[g, 4 + n], at_x(x, 1 - c)))

    one_head(0)
    plus((1, 2))
    one_head(1)
    att_send_own(0)
    minus((0, 3))
    plus((2, 2))
    one_head(2)
    minus((1, 3))
    one_head(3)
    att_send_own(1)
    plus((3, 2), (4, 2))
    minus((2, 3))
    one_head(4)
    att_pass(0)
    minus((3, 3))
    one_head(5)
    att_send_own(2)
    plus((0, 3))
    minus((4, 3))
    one_head(6)
    att_pass(1)
    plus((1, 3))
    one_head(7)
    att_send_own(3)
    minus((0, 4))
    plus((2, 3))

    target = xl + 2 * c
    role = (y - target + 4) % 4

    def ra_copy(k, side):
        return pltpu.make_async_remote_copy(
            src_ref=pbuf[k].at[side * 256:(side + 1) * 256, :], dst_ref=rabuf[k],
            send_sem=ra_send.at[k, side], recv_sem=ra_recv.at[k],
            device_id=at_y(1 - 2 * side), device_id_type=MESH,
        )

    def rm_copy(k, side):
        return pltpu.make_async_remote_copy(
            src_ref=pbuf[k], dst_ref=rmbuf[k].at[side],
            send_sem=rm_send.at[k, side], recv_sem=rm_recv.at[k, side],
            device_id=at_y(1 - 2 * side), device_id_type=MESH,
        )

    def rx_copy(k, d):
        j = (i + d) % 4
        return pltpu.make_async_remote_copy(
            src_ref=pbuf[k].at[pl.ds(pl.multiple_of(j * 128, 128), 128), :],
            dst_ref=final.at[:, OFFS[k]:OFFS[k] + WIDTHS[k]],
            send_sem=rx_send.at[k, d - 1], recv_sem=rx_recv.at[k],
            device_id=(z * 4 + j, head), device_id_type=MESH,
        )

    def reduce_first(k):
        w = wbuf[k]
        acc[k][...] = jnp.dot(
            att[0], w[:, 0].reshape(1024, WIDTHS[k]), preferred_element_type=F32
        ) + jnp.dot(att[1], w[:, 1].reshape(1024, WIDTHS[k]), preferred_element_type=F32)

        @pl.when(role == 2)
        def _():
            pbuf[k][...] = acc[k][...].astype(BF16)
            ra_copy(k, 0).start()
            ra_copy(k, 1).start()

    def reduce_second(k):
        for mine, side in ((3, 0), (1, 1)):
            @pl.when(role == mine)
            def _():
                here = slice(side * 256, (side + 1) * 256)
                there = slice((1 - side) * 256, (2 - side) * 256)
                pbuf[k][there, :] = acc[k][there, :].astype(BF16)
                ra_copy(k, side).wait_recv()
                pbuf[k][here, :] = (acc[k][here, :] + rabuf[k][...].astype(F32)).astype(BF16)
                rm_copy(k, side).start()

    def reduce_third(k):
        @pl.when(role == 0)
        def _():
            rm_copy(k, 0).wait_recv()
            rm_copy(k, 1).wait_recv()
            pbuf[k][...] = (acc[k][...] + rmbuf[k][0].astype(F32) + rmbuf[k][1].astype(F32)).astype(BF16)
            for d in (1, 2, 3):
                rx_copy(k, d).start()

    def reduce_last(k):
        cols = slice(OFFS[k], OFFS[k] + WIDTHS[k])

        @pl.when(role == 0)
        def _():
            out[:, cols] = pbuf[k][pl.ds(pl.multiple_of(i * 128, 128), 128), :]

        @pl.when(role != 0)
        def _():
            rx_copy(k, 1).wait_recv()
            out[:, cols] = final[:, cols]

    att_pass(2)
    minus((1, 4))
    plus((3, 3), (4, 3))
    att_pass(3)
    minus((2, 4))
    for g in range(4):
        for copy in att2[g]:
            copy.wait_recv()
    minus((3, 4), (4, 4))
    plus((0, 4))
    minus((0, 5))
    reduce_first(0)
    plus((1, 4))
    minus((1, 5))
    reduce_first(1)
    reduce_second(0)
    plus((2, 4))
    minus((2, 5))
    reduce_first(2)
    reduce_second(1)
    reduce_third(0)
    plus((3, 4))
    minus((3, 5))
    reduce_first(3)
    reduce_second(2)
    reduce_third(1)
    plus((4, 4))
    minus((4, 5))
    reduce_first(4)
    reduce_second(3)
    reduce_third(2)
    reduce_second(4)
    reduce_third(3)
    reduce_third(4)
    for k in range(PARTS):
        reduce_last(k)

    for copy in sent:
        copy.wait_send()

    @pl.when(role == 2)
    def _():
        for k in range(PARTS):
            ra_copy(k, 0).wait_send()
            ra_copy(k, 1).wait_send()

    for mine, side in ((3, 0), (1, 1)):
        @pl.when(role == mine)
        def _():
            for k in range(PARTS):
                rm_copy(k, side).wait_send()

    @pl.when(role == 0)
    def _():
        for k in range(PARTS):
            for d in (1, 2, 3):
                rx_copy(k, d).wait_send()


def body(q_latent, kv_latent, q_gain, kv_gain, q_up, kv_up, out_proj, segment_ids, trace_limit):
    start_tab, step_tab = tables()
    any_spec = pl.BlockSpec(memory_space=pl.ANY)
    dma = pltpu.SemaphoreType.DMA
    scratch = [
        pltpu.VMEM((ROWS, Q_RANK), BF16),
        pltpu.VMEM((KV_RANK + ROPE, ROWS), BF16),
        pltpu.VMEM((Q_RANK // 128, 128), F32),
        pltpu.VMEM((1, KV_RANK), F32),
        pltpu.VMEM((Q_RANK, HEADS * (NOPE + ROPE)), BF16),
        pltpu.VMEM((KV_RANK, HEADS * 256), BF16),
        pltpu.VMEM((32, 128), jnp.int32),
        pltpu.VMEM((32, 256), F32),
        pltpu.VMEM((128, 256), F32),
        pltpu.VMEM((12 * ROWS, LAT), BF16),
        pltpu.VMEM((12 * ROWS, HEADS * 256), BF16),
        pltpu.VMEM((ROWS, WINDOW), F32),
        pltpu.VMEM((HEADS, ROWS, 256), BF16),
        pltpu.VMEM((2, 4 * ROWS, HEADS * 128), BF16),
        pltpu.VMEM((ROWS, BLOCK), BF16),
        [pltpu.VMEM((8, 2, 128, w), BF16) for w in WIDTHS],
        [pltpu.VMEM((512, w), BF16) for w in WIDTHS],
        [pltpu.VMEM((256, w), BF16) for w in WIDTHS],
        [pltpu.VMEM((2, 512, w), BF16) for w in WIDTHS],
        [pltpu.VMEM((512, w), F32) for w in WIDTHS],
        dma((9,)),
        dma((PARTS,)),
        dma((PARTS, 7)),
        dma((PARTS, 7)),
        dma((PARTS, 2, 4)),
        dma((PARTS, 2, 4)),
        dma((3, 5)),
        dma((3, 5)),
        dma((4, 8)),
        dma((4, 8)),
        dma((PARTS, 2)),
        dma((PARTS,)),
        dma((PARTS, 2)),
        dma((PARTS, 2)),
        dma((PARTS, 3)),
        dma((PARTS,)),
    ]
    return pl.pallas_call(
        kernel,
        out_shape=jax.ShapeDtypeStruct((ROWS, BLOCK), BF16),
        in_specs=[any_spec] * 8 + [pl.BlockSpec(memory_space=pltpu.SMEM)] + [any_spec] * 2,
        out_specs=pl.BlockSpec(memory_space=pltpu.VMEM),
        scratch_shapes=scratch,
        compiler_params=pltpu.CompilerParams(
            collective_id=0, has_side_effects=True, vmem_limit_bytes=56 * 2**20
        ),
        name="latent_attention",
    )(
        q_latent, kv_latent.T, q_gain.reshape(Q_RANK // 128, 128), kv_gain.reshape(1, KV_RANK), q_up, kv_up,
        out_proj, segment_ids.reshape(32, 128), trace_limit, jnp.asarray(start_tab), jnp.asarray(step_tab),
    )


def solution(mesh):
    in_specs = (
        P("ctx", None),
        P("ctx", None),
        P(),
        P(),
        P(None, "head"),
        P(None, "head"),
        P(("head", "ctx"), None),
        P(),
        P(),
    )
    return jax.shard_map(body, mesh=mesh, in_specs=in_specs, out_specs=P("ctx", "head"), check_vma=False)
```

time: 275 us -> 75.9 us (0.28)
  the two profiles are of different devices: /device:TPU:65 before, /device:TPU:3 now
where the time goes in v2:
time: 75.9 us; the launch traced here: 75.8 us
  Pallas kernels  74.1 us (98%)
  local copies, waits for them, and re-layouts  1.65 us (2%)
    pallas_call x1, Pallas kernels, body(): pl.pallas_call(kernel, out_shape=jax.ShapeDtypeStruct((ROWS, BLOCK), BF16...  74.1 us
    unnamed x1, local copies, waits for them, and re-layouts  1.65 us

profile of v2, /device:TPU:3, one launch (start us, length us, event | category | flops | bytes accessed | tf_op | source)
XLA Modules:
  0.0 75.8 jit_solution(2516656537724003139)
XLA Ops:
  0.0 74.1 %latent_attention.1 = bf16[128,896]{1,0:T(8,128)(2,1)} custom-call(bf16[128,1536]{1,0:T(8,128)(2,1)} %q_latent.1, bf16[576,128]{1,0:T(8,128)(2,1)} %bitcast.4, f32[12,128]{1,0:T(8,128)} %bitcast.6, f32[1,512]{1,0:T(1,128)} %bitcast.7, bf16[1536,1536]{1,0:T(8,128)(2,1)} %q_up.1, bf16[512,2048]{1,0:T(8,128)(2,1)} %kv_up.1, bf16[32,7168]{1,0:T(8,128)(2,1)} %out_proj.1, ...), custom_call_target="tpu_custom_call" | custom-call | tf_op jit(solution)/shard_map/latent_attention/pallas_call | solution.py:506
  74.1 1.6 %copy.13 = bf16[128,896]{1,0:T(8,128)(2,1)} copy(bf16[128,896]{1,0:T(8,128)(2,1)} %latent_attention.1) | data formatting | bytes 458752
